TPU v7x, 512 devices: a whole 4x4x16 slice. The times are simulated.
512 devices in a mesh: expert: 8 (over z_lo, core), dp: 64 (over z_hi, x, y).
Axes of the slice: x: 4, y: 4, z: 16 (z_hi: 4, z_lo: 4; z = z_hi * 4 + z_lo), core: 2. Of those that a mesh axis runs over, the one named last changes fastest.
Arguments:
- x_rows: bfloat16 [8, 64, 8, 2, 3072], P('expert', 'dp'), may hold values from -6 to 6
- cot_rows: bfloat16 [8, 64, 8, 2, 3072], P('expert', 'dp'), may hold values from -3 to 3
- counts: int32 [8, 64, 8], P(None, 'dp'), may hold values from 0 to 2, as said below
- w_gate: bfloat16 [8, 3072, 8192], P('expert', None, 'dp'), may hold values from -0.109375 to 0.109375
- w_up: bfloat16 [8, 3072, 8192], P('expert', None, 'dp'), may hold values from -0.109375 to 0.109375
- w_down: bfloat16 [8, 8192, 3072], P('expert', 'dp'), may hold values from -0.0625 to 0.0625
- kept_blocks: int32 [8], P('expert'), may hold values from 16 to 64
- block_rank: int32 [8, 64], P('expert', 'dp'), may hold values from 0 to 63, each once within a row
Outputs:
- grad_rows: bfloat16 [8, 64, 8, 2, 3072], P('expert', 'dp')
- grad_gate: bfloat16 [8, 3072, 8192], P('expert', None, 'dp')
- grad_up: bfloat16 [8, 3072, 8192], P('expert', None, 'dp')
- grad_down: bfloat16 [8, 8192, 3072], P('expert', 'dp')
Inputs may be any that keep to these rules, and one draw needn't show every extreme that they name: The live slots of a source's buffer for an expert are its first ones. For every expert e and index d the sum over sources s of counts[s, d, e] is at most 4, and it equals 4 for every d of some expert.
All inputs are finite; a program needn't handle non-finite values.
Results may differ from a plain program's by a relative error of at most 0.005.
Values may be sent and summed in bfloat16 or wider, within the bound.
No kernel may reach another device: no remote copies, remote signals or barrier semaphores. Data moves between devices by JAX's collectives and lax.ppermute only.
A program may use at most 64 MiB of HBM per device.

v0:
```python
import jax
import jax.numpy as jnp
from jax import lax
from jax.sharding import PartitionSpec as P

LIVE = 4


def compact_matrix(slot_counts, live_rows, capacity):
    sources = slot_counts.shape[0]
    within_slot = jnp.tile(jnp.arange(capacity, dtype=jnp.int32), sources)
    count_slot = jnp.repeat(slot_counts, capacity)
    offsets = jnp.repeat(jnp.cumsum(slot_counts) - slot_counts, capacity)
    target = offsets + within_slot
    alive = within_slot < count_slot
    row_index = jnp.arange(live_rows, dtype=jnp.int32)[:, None]
    return ((row_index == target[None, :]) & alive[None, :]).astype(jnp.bfloat16)


def contract(left, right, left_dim, right_dim):
    return lax.dot_general(
        left, right, (((left_dim,), (right_dim,)), ((), ())), preferred_element_type=jnp.float32
    )


def body(x_rows, cot_rows, counts, w_gate, w_up, w_down, kept_blocks, block_rank):
    expert_count = x_rows.shape[2]
    capacity = x_rows.shape[3]
    model_width = x_rows.shape[4]
    slot_rows = x_rows.reshape(expert_count, capacity, model_width)
    slot_cots = cot_rows.reshape(expert_count, capacity, model_width)
    my_expert = lax.axis_index("expert")
    picked = jnp.arange(expert_count, dtype=jnp.int32)[None, :] == my_expert
    own_counts = jnp.sum(jnp.where(picked, counts[:, 0, :], 0), axis=1)
    chooser = compact_matrix(own_counts, LIVE, capacity)

    def pack_rows(received):
        flat_rows = received.reshape(-1, model_width)
        return jnp.dot(chooser, flat_rows, preferred_element_type=jnp.float32).astype(jnp.bfloat16)

    got_rows, got_cots = (
        lax.all_to_all(slot_rows, "expert", split_axis=0, concat_axis=0, tiled=True),
        lax.all_to_all(slot_cots, "expert", split_axis=0, concat_axis=0, tiled=True),
    )
    group_rows, group_cots = (
        lax.all_gather(pack_rows(got_rows), "dp", axis=0, tiled=True),
        lax.all_gather(pack_rows(got_cots), "dp", axis=0, tiled=True),
    )
    gate_weight = w_gate[0]
    up_weight = w_up[0]
    down_weight = w_down[0]
    keep_mask = (block_rank.reshape(()) < kept_blocks.reshape(())).astype(jnp.float32)
    gate_pre = jnp.dot(group_rows, gate_weight, preferred_element_type=jnp.float32)
    up_pre = jnp.dot(group_rows, up_weight, preferred_element_type=jnp.float32)
    sigmoid_gate = jax.nn.sigmoid(gate_pre)
    activated = gate_pre * sigmoid_gate
    hidden = (activated * up_pre * keep_mask).astype(jnp.bfloat16)
    hidden_grad = contract(group_cots, down_weight, 1, 1)
    up_grad = (hidden_grad * activated * keep_mask).astype(jnp.bfloat16)
    gate_grad = (
        hidden_grad * up_pre * sigmoid_gate * (1.0 + gate_pre * (1.0 - sigmoid_gate)) * keep_mask
    ).astype(jnp.bfloat16)
    grad_down = contract(hidden, group_cots, 0, 0).astype(jnp.bfloat16)
    grad_gate = contract(group_rows, gate_grad, 0, 0).astype(jnp.bfloat16)
    grad_up = contract(group_rows, up_grad, 0, 0).astype(jnp.bfloat16)
    whole_term = contract(gate_grad, gate_weight, 1, 1) + contract(up_grad, up_weight, 1, 1)
    row_grads = lax.psum_scatter(whole_term, "dp", scatter_dimension=0, tiled=True)
    row_grads = row_grads.astype(jnp.bfloat16)
    slot_grads = contract(chooser, row_grads, 0, 0).astype(jnp.bfloat16)
    slot_grads = slot_grads.reshape(expert_count, capacity, model_width)
    returned = lax.all_to_all(slot_grads, "expert", split_axis=0, concat_axis=0, tiled=True)
    grad_rows = returned.reshape(1, 1, expert_count, capacity, model_width)
    return (grad_rows, grad_gate[None], grad_up[None], grad_down[None])


def solution(mesh):
    in_specs = (
        P("expert", "dp", None, None, None),
        P("expert", "dp", None, None, None),
        P(None, "dp", None),
        P("expert", None, "dp"),
        P("expert", None, "dp"),
        P("expert", "dp", None),
        P("expert"),
        P("expert", "dp"),
    )
    out_specs = (
        P("expert", "dp", None, None, None),
        P("expert", None, "dp"),
        P("expert", None, "dp"),
        P("expert", "dp", None),
    )
    return jax.shard_map(body, mesh=mesh, in_specs=in_specs, out_specs=out_specs, check_vma=False)
```

profile of v0, /device:TPU:1, one launch (start us, length us, event | category | flops | bytes accessed | tf_op | source)
XLA Modules:
  0.0 771.1 jit_solution(15349936523839550636)
XLA Ops:
  7.2 10.3 %all-to-all-start.1 = ((bf16[8,2,3072]{2,1,0:T(2,128)(2,1)}), bf16[8,2,3072]{2,1,0:T(2,128)(2,1)S(1)}, u32[]{:S(2)}, u32[]{:S(2)}) async-start(bf16[8,2,3072]{2,1,0:T(2,128)(2,1)} %bitcast.50), calls=%async_computation.1 | async-start | bytes 196608 | tf_op jit(solution)/shard_map/all_to_all | solution.py:42
  17.5 0.8 select_reduce_fusion
  18.8 4.2 all-to-all-done.1
  23.0 0.7 fusion.4
  23.8 9.6 %all_to_all.15 = bf16[8,2,3072]{2,1,0:T(2,128)(2,1)S(1)} all-to-all(bf16[8,2,3072]{2,1,0:T(2,128)(2,1)} %bitcast.51), channel_id=1, replica_groups=mesh['expert'=8,'dp'=64] {'expert'}, dimensions={0} | all-to-all | bytes 196608 | tf_op jit(solution)/shard_map/all_to_all | solution.py:43
  33.5 0.7 fusion.3
  35.6 1.3 dynamic-slice
  37.5 93.3 %all-gather.7.cloned.1.call-done = bf16[64,4,3072]{2,1,0:T(4,128)(2,1)} async-done(((bf16[1,4,3072]{2,1,0:T(4,128)(2,1)}), bf16[64,4,3072]{2,1,0:T(4,128)(2,1)}) %all-gather.7.cloned.1.call-update) | async-done | bytes 1572880 | tf_op jit(solution)/shard_map/all_gather | solution.py:46
  130.8 2.7 reshape.98
  134.1 0.6 copy-done.2
  135.2 102.1 %all-gather.5.cloned.1.call-done = bf16[64,4,3072]{2,1,0:T(4,128)(2,1)} async-done(((bf16[1,4,3072]{2,1,0:T(4,128)(2,1)}), bf16[64,4,3072]{2,1,0:T(4,128)(2,1)}) %all-gather.5.cloned.1.call-update) | async-done | bytes 1572880 | tf_op jit(solution)/shard_map/all_gather | solution.py:47
  237.3 3.7 reshape.96
  241.0 2.2 multiply_convert_fusion.1
  243.2 1.5 fusion.1
  244.7 0.6 fusion.5
  245.3 2.3 convolution_add_fusion
  247.5 448.0 %all-reduce.2 = bf16[256,3072]{1,0:T(8,128)(2,1)} all-reduce(f32[256,3072]{1,0:T(8,128)} %convolution_add_fusion), channel_id=2, replica_groups=mesh['expert'=8,'dp'=64] {'dp'}, use_global_device_ids=true, to_apply=%region_2.3.clone | all-reduce | flops 786432 | bytes 4718592
  695.5 1.0 convolution_convert_fusion.3
  696.6 0.7 reshape.93
  697.3 60.9 %all-to-all-start.2 = ((bf16[8,2,3072]{2,1,0:T(2,128)(2,1)}), bf16[8,2,3072]{2,1,0:T(2,128)(2,1)S(1)}, u32[]{:S(2)}, u32[]{:S(2)}) async-start(bf16[8,2,3072]{2,1,0:T(2,128)(2,1)} %reshape.93), calls=%async_computation.2 | async-start | bytes 196608 | tf_op jit(solution)/shard_map/all_to_all | solution.py:71
  758.1 1.5 fusion
  759.6 1.3 fusion.2
  761.0 2.6 all-to-all-done.2
  763.6 0.6 copy.17
  (20 shorter events, 1.8 us)
Async XLA Ops:
  7.2 126.4 %copy-start = (bf16[1,3072,128]{2,1,0:T(8,128)(2,1)S(1)}, bf16[1,3072,128]{2,1,0:T(8,128)(2,1)}, u32[]{:S(2)}) copy-start(bf16[1,3072,128]{2,1,0:T(8,128)(2,1)} %param.11) | copy-start | bytes 2359300
  7.2 15.8 %all-to-all-start.1 = ((bf16[8,2,3072]{2,1,0:T(2,128)(2,1)}), bf16[8,2,3072]{2,1,0:T(2,128)(2,1)S(1)}, u32[]{:S(2)}, u32[]{:S(2)}) async-start(bf16[8,2,3072]{2,1,0:T(2,128)(2,1)} %bitcast.50), calls=%async_computation.1 | async-start | bytes 196608 | tf_op jit(solution)/shard_map/all_to_all | solution.py:42
  17.5 113.3 %all-gather.7.cloned.1.call-start = ((), (), s32[]{:S(2)}) async-start(), calls=%async_computation.4 | async-start | bytes 1597440 | tf_op jit(solution)/shard_map/all_gather | solution.py:46
  23.8 213.5 %all-gather.5.cloned.1.call-start = ((), (), s32[]{:S(2)}) async-start(), calls=%async_computation.3 | async-start | bytes 1597440 | tf_op jit(solution)/shard_map/all_gather | solution.py:47
  133.5 1.1 copy-start.2
  697.3 66.3 %all-to-all-start.2 = ((bf16[8,2,3072]{2,1,0:T(2,128)(2,1)}), bf16[8,2,3072]{2,1,0:T(2,128)(2,1)S(1)}, u32[]{:S(2)}, u32[]{:S(2)}) async-start(bf16[8,2,3072]{2,1,0:T(2,128)(2,1)} %reshape.93), calls=%async_computation.2 | async-start | bytes 196608 | tf_op jit(solution)/shard_map/all_to_all | solution.py:71
  758.1 1.5 copy-start.1
Sparse Core Ops, SparseCore 0:
  23.9 106.8 all-gather.6
  135.4 101.8 all-gather.4
where the time goes:
time: 772 us; the launch traced here: 771 us
  blocking collectives  458 us (59%)
  waiting for transfers between devices  202 us (26%)
  starting transfers between devices  71.2 us (9%)
  between operations  16.1 us (2%)
  matrix products  13 us (2%)
  local copies, waits for them, and re-layouts  9.87 us (1%)
    unnamed x1, blocking collectives  448 us
    all_gather x1, waiting for transfers between devices, body(): lax.all_gather(pack_rows(got_cots), 'dp', axis=0, tiled=True)  102 us
    all_gather x1, waiting for transfers between devices, body(): lax.all_gather(pack_rows(got_rows), 'dp', axis=0, tiled=True)  93.3 us
    all_to_all x1, starting transfers between devices, body(): lax.all_to_all(slot_grads, 'expert', split_axis=0, concat_axis=0, tiled=T...  60.9 us
  transfers between devices with their start and end apart: 4, of which 4 were waited for; matrix products, arithmetic and copies ran while one was open for 1% of the time, Pallas kernels for 0%

commit v1 on v0

--- a/solution.py
+++ b/solution.py
@@ -43,7 +43,10 @@
         lax.all_to_all(slot_cots, "expert", split_axis=0, concat_axis=0, tiled=True),
     )
     group_rows, group_cots = (
-        lax.all_gather(pack_rows(got_rows), "dp", axis=0, tiled=True),
+        jnp.concatenate(
+            lax.all_to_all(jnp.stack([pack_rows(got_rows)] * lax.axis_size("dp")), "dp", 0, 0),
+            axis=0,
+        ),
         lax.all_gather(pack_rows(got_cots), "dp", axis=0, tiled=True),
     )
     gate_weight = w_gate[0]

time: 772 us -> 737 us (0.955)
  waiting for transfers between devices: 202 us -> 160 us
    all_gather x1 -> x0, waiting for transfers between devices: 93.3 us -> none  [body(): lax.all_gather(pack_rows(got_rows), 'dp', axis=0, tiled=True)]
    all_gather x1, waiting for transfers between devices: 102 us -> 148 us  [body(): lax.all_gather(pack_rows(got_cots), 'dp', axis=0, tiled=True)]
    all_to_all x0 -> x2, starting transfers between devices: none -> 19.9 us  [the longest x1 15.8 us: body(): lax.all_to_all(jnp.stack([pack_rows(got_rows)] * lax.axis_size('dp')), 'd...]
    all_to_all x1, starting transfers between devices: 60.9 us -> 47.6 us  [body(): lax.all_to_all(slot_grads, 'expert', split_axis=0, concat_axis=0, tiled=T...]
    unnamed x1, blocking collectives: 448 us -> 458 us
    all_to_all x1 -> x0, blocking collectives: 9.62 us -> none  [body(): lax.all_to_all(slot_cots, 'expert', split_axis=0, concat_axis=0, tiled=True)]
  transfers between devices with their start and end apart: 4 -> 5, of which waited for: 4 -> 4; matrix products, arithmetic and copies ran while one was open for 1% -> 1% of each run, Pallas kernels for 0% -> 0%
where the time goes in v1:
time: 737 us
  blocking collectives  458 us (62%)
  waiting for transfers between devices  160 us (22%)
  starting transfers between devices  77.9 us (11%)
  between operations  16.1 us (2%)
  local copies, waits for them, and re-layouts  12.5 us (2%)
  matrix products  10.7 us (1%)
    unnamed x1, blocking collectives  458 us
    all_gather x1, waiting for transfers between devices, body(): lax.all_gather(pack_rows(got_cots), 'dp', axis=0, tiled=True)  148 us
    all_to_all x1, starting transfers between devices, body(): lax.all_to_all(slot_grads, 'expert', split_axis=0, concat_axis=0, tiled=T...  47.6 us
    all_to_all x1, starting transfers between devices, body(): lax.all_to_all(jnp.stack([pack_rows(got_rows)] * lax.axis_size('dp')), 'd...  15.8 us
  transfers between devices with their start and end apart: 5, of which 4 were waited for; matrix products, arithmetic and copies ran while one was open for 1% of the time, Pallas kernels for 0%

profile of v1, /device:TPU:1, one launch (start us, length us, event | category | flops | bytes accessed | tf_op | source)
XLA Modules:
  0.0 736.5 jit_solution(17040511100981461106)
XLA Ops:
  7.2 10.3 %all-to-all-start.1 = ((bf16[8,2,3072]{2,1,0:T(2,128)(2,1)}), bf16[8,2,3072]{2,1,0:T(2,128)(2,1)S(1)}, u32[]{:S(2)}, u32[]{:S(2)}) async-start(bf16[8,2,3072]{2,1,0:T(2,128)(2,1)} %bitcast.48), calls=%async_computation.1 | async-start | bytes 196608 | tf_op jit(solution)/shard_map/all_to_all | solution.py:42
  17.5 0.8 select_reduce_fusion
  18.6 4.3 all-to-all-done.1
  23.0 4.1 all-to-all-start
  27.4 5.2 all-to-all-done
  32.6 1.6 stack.2
  34.2 15.8 %all-to-all-start.2 = ((bf16[64,4,3072]{2,1,0:T(4,128)(2,1)}), bf16[64,4,3072]{2,1,0:T(4,128)(2,1)}, u32[]{:S(2)}, u32[]{:S(2)}) async-start(bf16[64,4,3072]{2,1,0:T(4,128)(2,1)} %stack.2), calls=%async_computation.2 | async-start | bytes 3145728 | tf_op jit(solution)/shard_map/all_to_all | solution.py:47
  50.0 0.7 fusion.3
  52.1 1.3 dynamic-slice
  54.0 147.9 %all-gather.3.cloned.1.call-done = bf16[64,4,3072]{2,1,0:T(4,128)(2,1)} async-done(((bf16[1,4,3072]{2,1,0:T(4,128)(2,1)}), bf16[64,4,3072]{2,1,0:T(4,128)(2,1)}) %all-gather.3.cloned.1.call-update) | async-done | bytes 1572880 | tf_op jit(solution)/shard_map/all_gather | solution.py:50
  202.0 3.7 reshape.102
  205.7 2.7 reshape.96
  210.2 0.8 copy-done.1
  211.2 0.6 multiply_convert_fusion.1
  211.8 1.5 fusion.1
  213.8 2.2 convolution_add_fusion
  216.1 458.1 %all-reduce.2 = bf16[256,3072]{1,0:T(8,128)(2,1)} all-reduce(f32[256,3072]{1,0:T(8,128)} %convolution_add_fusion), channel_id=2, replica_groups=mesh['expert'=8,'dp'=64] {'dp'}, use_global_device_ids=true, to_apply=%region_2.3.clone | all-reduce | flops 786432 | bytes 4718592
  674.2 1.0 convolution_convert_fusion.3
  675.2 0.7 reshape.99
  675.9 47.6 %all-to-all-start.3 = ((bf16[8,2,3072]{2,1,0:T(2,128)(2,1)}), bf16[8,2,3072]{2,1,0:T(2,128)(2,1)S(1)}, u32[]{:S(2)}, u32[]{:S(2)}) async-start(bf16[8,2,3072]{2,1,0:T(2,128)(2,1)} %reshape.99), calls=%async_computation.3 | async-start | bytes 196608 | tf_op jit(solution)/shard_map/all_to_all | solution.py:74
  723.5 1.5 fusion
  725.0 1.3 fusion.2
  726.4 2.7 all-to-all-done.3
  729.0 0.6 copy.17
  (25 shorter events, 3.3 us)
Async XLA Ops:
  7.2 201.3 %copy-start = (bf16[1,3072,128]{2,1,0:T(8,128)(2,1)S(1)}, bf16[1,3072,128]{2,1,0:T(8,128)(2,1)}, u32[]{:S(2)}) copy-start(bf16[1,3072,128]{2,1,0:T(8,128)(2,1)} %param.11) | copy-start | bytes 2359300
  7.2 15.8 %all-to-all-start.1 = ((bf16[8,2,3072]{2,1,0:T(2,128)(2,1)}), bf16[8,2,3072]{2,1,0:T(2,128)(2,1)S(1)}, u32[]{:S(2)}, u32[]{:S(2)}) async-start(bf16[8,2,3072]{2,1,0:T(2,128)(2,1)} %bitcast.48), calls=%async_computation.1 | async-start | bytes 196608 | tf_op jit(solution)/shard_map/all_to_all | solution.py:42
  23.0 9.6 %all-to-all-start = ((bf16[8,2,3072]{2,1,0:T(2,128)(2,1)}), bf16[8,2,3072]{2,1,0:T(2,128)(2,1)S(1)}, u32[]{:S(2)}, u32[]{:S(2)}) async-start(bf16[8,2,3072]{2,1,0:T(2,128)(2,1)} %bitcast.49), calls=%async_computation | async-start | bytes 196608 | tf_op jit(solution)/shard_map/all_to_all | solution.py:43
  34.2 171.5 %all-to-all-start.2 = ((bf16[64,4,3072]{2,1,0:T(4,128)(2,1)}), bf16[64,4,3072]{2,1,0:T(4,128)(2,1)}, u32[]{:S(2)}, u32[]{:S(2)}) async-start(bf16[64,4,3072]{2,1,0:T(4,128)(2,1)} %stack.2), calls=%async_computation.2 | async-start | bytes 3145728 | tf_op jit(solution)/shard_map/all_to_all | solution.py:47
  49.9 152.0 %all-gather.3.cloned.1.call-start = ((), (), s32[]{:S(2)}) async-start(), calls=%async_computation.4 | async-start | bytes 1597440 | tf_op jit(solution)/shard_map/all_gather | solution.py:50
  208.4 1.1 copy-start.3
  209.6 1.4 copy-start.1
  209.6 1.6 copy-start.4
  675.9 53.2 %all-to-all-start.3 = ((bf16[8,2,3072]{2,1,0:T(2,128)(2,1)}), bf16[8,2,3072]{2,1,0:T(2,128)(2,1)S(1)}, u32[]{:S(2)}, u32[]{:S(2)}) async-start(bf16[8,2,3072]{2,1,0:T(2,128)(2,1)} %reshape.99), calls=%async_computation.3 | async-start | bytes 196608 | tf_op jit(solution)/shard_map/all_to_all | solution.py:74
  723.5 1.5 copy-start.2
Sparse Core Ops, SparseCore 0:
  55.4 146.4 all-gather.2
